TPU v7x, 128 devices: a whole 4x4x4 slice. The times are simulated.
128 devices in a mesh: prompt: 4 (over z_hi, core), sample: 32 (over x, z_lo, y).
Axes of the slice: x: 4, y: 4, z: 4 (z_hi: 2, z_lo: 2; z = z_hi * 2 + z_lo), core: 2. Of those that a mesh axis runs over, the one named last changes fastest.
Arguments:
- answer_qkv: bfloat16 [4, 4096, 3, 4096], P('prompt', 'sample'), may hold values from -80 to 80
- prefix_kv: bfloat16 [4, 2048, 2, 4096], P(None, 'prompt', None, 'sample'), may hold values from -6 to 6
- reveal_qkv: bfloat16 [4, 512, 3, 4096], P('prompt', 'sample'), may hold values from -4 to 4
- reveal_places: int32 [4, 32, 16], P('prompt', 'sample'), may hold values from 0 to 127, as said below
Outputs:
- attended_one: bfloat16 [4, 4096, 4096], P('prompt', 'sample')
- attended_two: bfloat16 [4, 4096, 4096], P('prompt', 'sample')
Inputs may be any that keep to these rules, and one draw needn't show every extreme that they name: `reveal_places`: within each prompt and segment the 16 entries are distinct positions of that segment.
All inputs are finite; a program needn't handle non-finite values.
Results may differ from a plain program's by a relative error of at most 0.0095.
Values may be sent and summed in bfloat16 or wider, within the bound.
No kernel may reach another device: no remote copies, remote signals or barrier semaphores. Data moves between devices by JAX's collectives and lax.ppermute only.
A program may use at most 128 MiB of HBM per device.

v0:
```python
import functools
import math

import jax
import jax.numpy as jnp
from jax import lax
from jax.experimental import pallas as pl
from jax.experimental.pallas import tpu as pltpu
from jax.sharding import PartitionSpec as P

HEAD_DIM = 128
ANS = 1024
SEG = 128
REV = 16
KEPT = SEG - REV
ROWS = SEG + REV
SEGS = ANS // SEG
QUERIES = SEGS * ROWS
PREFIX = 2048
CHUNK = 512
RATE = math.log2(math.e) / math.sqrt(HEAD_DIM)
LIMIT = 100.0
AUG = HEAD_DIM + 16
NT = (((1,), (1,)), ((), ()))
FLIPS = (3, 2, 1)
VMEM_LIMIT = 63 * 2**20
FIRST = 128
SPAN = 4
PREFIX_COST = 60_000_000_000


def scores_of(keys, queries):
    return lax.dot_general(keys, queries, NT, preferred_element_type=jnp.float32)


def fold_max(scores):
    return jnp.max(scores.reshape(-1, 8, scores.shape[1]), axis=0)


def weigh(scores, reference_row):
    return jnp.exp2((scores - reference_row) * RATE).astype(jnp.bfloat16)


def attend_kernel(qkv_ref, kp_ref, vpt_ref, out_ref, queries_ref):
    queries_ref[: SEGS * SEG] = qkv_ref[:, 0, :SEG].reshape(SEGS * SEG, HEAD_DIM)
    queries_ref[SEGS * SEG :] = qkv_ref[:, 0, SEG:].reshape(SEGS * REV, HEAD_DIM)

    def answer_rows(kind, segs, rows):
        picked = qkv_ref[segs, kind, rows]
        return picked.reshape(picked.shape[0] * picked.shape[1], HEAD_DIM)

    def weighted(values, weights):
        ones = jnp.ones((AUG - HEAD_DIM, values.shape[0]), jnp.bfloat16)
        turned = jnp.concatenate([values.T, ones], axis=0)
        return jnp.dot(turned, weights, preferred_element_type=jnp.float32)

    def attend(common_row, one_row, two_row, scale_one, scale_two):
        queries = queries_ref[...]
        total = None
        common_max = None
        for start in range(0, PREFIX, CHUNK):
            scores = scores_of(kp_ref[start : start + CHUNK], queries)
            folded = fold_max(scores)
            common_max = folded if common_max is None else jnp.maximum(common_max, folded)
            part = jnp.dot(
                vpt_ref[:, start : start + CHUNK],
                weigh(scores, common_row),
                preferred_element_type=jnp.float32,
            )
            total = part if total is None else total + part
        for start in range(0, SEGS, SPAN):
            segs = slice(start, start + SPAN)
            scores = scores_of(answer_rows(1, segs, slice(0, KEPT)), queries)
            common_max = jnp.maximum(common_max, fold_max(scores))
            total += weighted(answer_rows(2, segs, slice(0, KEPT)), weigh(scores, common_row))

        def step(rows, row, scale):
            scores = scores_of(answer_rows(1, slice(0, SEGS), rows), queries)
            own = weighted(answer_rows(2, slice(0, SEGS), rows), weigh(scores, row))
            own += total if scale is None else total * scale
            return own[:HEAD_DIM] * (1.0 / own[HEAD_DIM : HEAD_DIM + 1]), fold_max(scores)

        one, one_max = step(slice(KEPT, SEG), one_row, scale_one)
        two, two_max = step(slice(SEG, ROWS), two_row, scale_two)
        renewed = two[:, SEGS * SEG :]
        lane = lax.broadcasted_iota(jnp.int32, (HEAD_DIM, SEG), 1)
        for seg in range(SEGS):
            lanes = slice(seg * SEG, (seg + 1) * SEG)
            out_ref[seg, 0] = one[:, lanes].astype(jnp.bfloat16)
            shift = (KEPT - seg * REV) % SEG
            moved = pltpu.roll(renewed, shift, 1) if shift else renewed
            out_ref[seg, 1] = jnp.where(lane < KEPT, two[:, lanes], moved).astype(jnp.bfloat16)
        return common_max, one_max, two_max

    first = scores_of(kp_ref[:FIRST], queries_ref[...])
    start_row = jnp.max(first, axis=0, keepdims=True)
    common_max, one_max, two_max = attend(start_row, start_row, start_row, None, None)
    largest = jnp.maximum(common_max, jnp.maximum(one_max, two_max))
    excess = jnp.max(largest - start_row) * RATE

    @pl.when(excess > LIMIT)
    def _():
        common_row = jnp.max(common_max, axis=0, keepdims=True)
        one_row = jnp.maximum(common_row, jnp.max(one_max, axis=0, keepdims=True))
        two_row = jnp.maximum(common_row, jnp.max(two_max, axis=0, keepdims=True))
        attend(
            common_row,
            one_row,
            two_row,
            jnp.exp2((common_row - one_row) * RATE),
            jnp.exp2((common_row - two_row) * RATE),
        )


def attend(qkv, prefix_keys, prefix_values):
    samples = qkv.shape[0] // SEGS
    whole = lambda i: (0, 0)
    per = lambda i: (i, 0, 0, 0)
    return pl.pallas_call(
        attend_kernel,
        grid=(samples,),
        in_specs=[
            pl.BlockSpec((SEGS, 3, ROWS, HEAD_DIM), per),
            pl.BlockSpec((PREFIX, HEAD_DIM), whole),
            pl.BlockSpec((AUG, PREFIX), whole),
        ],
        out_specs=pl.BlockSpec((SEGS, 2, HEAD_DIM, SEG), per),
        out_shape=jax.ShapeDtypeStruct((samples * SEGS, 2, HEAD_DIM, SEG), jnp.bfloat16),
        scratch_shapes=[pltpu.VMEM((QUERIES, HEAD_DIM), jnp.bfloat16)],
        compiler_params=pltpu.CompilerParams(vmem_limit_bytes=VMEM_LIMIT),
        cost_estimate=pl.CostEstimate(
            flops=14_000_000_000, bytes_accessed=7_000_000, transcendentals=15_000_000
        ),
        name="attend",
    )(qkv, prefix_keys, prefix_values)


def place_kernel(heads, turned_ref, select_ref, one_ref, two_ref):
    for step, ref in enumerate((one_ref, two_ref)):
        ref[0] = lax.dot_general(
            select_ref[...],
            turned_ref[:, step].reshape(heads * HEAD_DIM, SEG),
            NT,
            preferred_element_type=jnp.float32,
        ).astype(jnp.bfloat16)


def place_outputs(turned, select):
    heads = 16
    count = turned.shape[0]
    shape = jax.ShapeDtypeStruct((1, SEG, count * HEAD_DIM), jnp.bfloat16)
    spec = pl.BlockSpec((1, SEG, heads * HEAD_DIM), lambda i: (0, 0, i))
    return pl.pallas_call(
        functools.partial(place_kernel, heads),
        grid=(count // heads,),
        in_specs=[
            pl.BlockSpec((heads, 2, HEAD_DIM, SEG), lambda i: (i, 0, 0, 0)),
            pl.BlockSpec((SEG, SEG), lambda i: (0, 0)),
        ],
        out_specs=[spec, spec],
        out_shape=[shape, shape],
        compiler_params=pltpu.CompilerParams(vmem_limit_bytes=VMEM_LIMIT),
        name="place",
    )(turned, select)


def row_order(places):
    diagonal = lax.broadcasted_iota(jnp.int32, (REV, REV), 0) == lax.broadcasted_iota(
        jnp.int32, (REV, REV), 1
    )
    column = jnp.sum(jnp.where(diagonal, places, 0), axis=1, keepdims=True)
    rows = lax.broadcasted_iota(jnp.int32, (REV, SEG), 1)
    hits = jnp.where(column == rows, 1, 0)
    below = jnp.where(column < rows, 1, 0)
    rank = rows[:1] - jnp.sum(below, axis=0, keepdims=True)
    rank = jnp.where(jnp.sum(hits, axis=0, keepdims=True) > 0, -1, rank)
    kept = jnp.where(lax.broadcasted_iota(jnp.int32, (KEPT, SEG), 0) == rank, 1, 0)
    return jnp.concatenate([kept, hits], axis=0).astype(jnp.float32)


def prefix_copies(prefix_ref, part_refs, sems):
    me = lax.axis_index("prompt")
    return [
        pltpu.make_async_copy(prefix_ref.at[me ^ flip], ref, sems.at[index])
        for index, (flip, ref) in enumerate(zip(FLIPS, part_refs))
    ]


def pack_kernel(
    heads, places_ref, rows_ref, reveal_ref, prefix_ref, out_ref, select_ref, *rest
):
    *part_refs, order_ref, sems = rest
    copies = prefix_copies(prefix_ref, part_refs, sems)

    @pl.when(pl.program_id(0) == 0)
    def _():
        for copy in copies:
            copy.start()
        order = row_order(places_ref[...])
        order_ref[...] = order.astype(jnp.bfloat16)
        select_ref[...] = order.T.astype(jnp.bfloat16)

    for kind in range(3):
        moved = jnp.dot(order_ref[...], rows_ref[0, kind], preferred_element_type=jnp.float32)
        moved = moved.astype(jnp.bfloat16)
        for head in range(heads):
            lanes = slice(head * HEAD_DIM, (head + 1) * HEAD_DIM)
            out_ref[head, kind, :SEG] = moved[:, lanes]
            out_ref[head, kind, SEG:] = reveal_ref[0, kind, :, lanes]

    @pl.when(pl.program_id(0) == pl.num_programs(0) - 1)
    def _():
        for copy in copies:
            copy.wait()


def pack(places, rows, reveal, prefix):
    heads = 16
    count = rows.shape[3] // HEAD_DIM
    width = heads * HEAD_DIM
    part = jax.ShapeDtypeStruct(prefix.shape[1:], jnp.bfloat16)
    return pl.pallas_call(
        functools.partial(pack_kernel, heads),
        grid=(count // heads,),
        in_specs=[
            pl.BlockSpec((1, REV), lambda i: (0, 0)),
            pl.BlockSpec((1, 3, SEG, width), lambda i: (0, 0, 0, i)),
            pl.BlockSpec((1, 3, REV, width), lambda i: (0, 0, 0, i)),
            pl.BlockSpec(memory_space=pl.ANY),
        ],
        out_specs=[
            pl.BlockSpec((heads, 3, ROWS, HEAD_DIM), lambda i: (i, 0, 0, 0)),
            pl.BlockSpec((SEG, SEG), lambda i: (0, 0)),
        ]
        + [pl.BlockSpec(part.shape, lambda i: (0, 0, 0))] * len(FLIPS),
        out_shape=[
            jax.ShapeDtypeStruct((count, 3, ROWS, HEAD_DIM), jnp.bfloat16),
            jax.ShapeDtypeStruct((SEG, SEG), jnp.bfloat16),
        ]
        + [part] * len(FLIPS),
        scratch_shapes=[
            pltpu.VMEM((SEG, SEG), jnp.bfloat16),
            pltpu.SemaphoreType.DMA((len(FLIPS),)),
        ],
        compiler_params=pltpu.CompilerParams(vmem_limit_bytes=VMEM_LIMIT),
        name="pack",
    )(places, rows, reveal, prefix)


def prefix_kernel(*refs):
    *parts, prefix_ref, keys_ref, values_ref, own_ref, sem = refs
    copy = pltpu.make_async_copy(prefix_ref.at[lax.axis_index("prompt")], own_ref, sem)
    copy.start()
    values_ref[HEAD_DIM:] = jnp.ones((AUG - HEAD_DIM, PREFIX), jnp.bfloat16)
    count = own_ref.shape[0]
    for index, part in enumerate((*parts, own_ref)):
        if part is own_ref:
            copy.wait()
        span = slice(index * count, (index + 1) * count)
        keys_ref[span] = part[:, 0]
        values_ref[:HEAD_DIM, span] = part[:, 1].T


def arrange_prefix(parts, prefix):
    vmem = pl.BlockSpec(memory_space=pltpu.VMEM)
    return pl.pallas_call(
        prefix_kernel,
        in_specs=[vmem] * len(parts) + [pl.BlockSpec(memory_space=pl.ANY)],
        out_specs=[vmem] * 2,
        out_shape=[
            jax.ShapeDtypeStruct((PREFIX, HEAD_DIM), jnp.bfloat16),
            jax.ShapeDtypeStruct((AUG, PREFIX), jnp.bfloat16),
        ],
        scratch_shapes=[
            pltpu.VMEM(prefix.shape[1:], jnp.bfloat16),
            pltpu.SemaphoreType.DMA,
        ],
        compiler_params=pltpu.CompilerParams(vmem_limit_bytes=VMEM_LIMIT),
        cost_estimate=pl.CostEstimate(
            flops=PREFIX_COST, bytes_accessed=2_000_000, transcendentals=0
        ),
        name="prefix",
    )(*parts, prefix)


def exchange(array):
    return lax.all_to_all(array, "sample", split_axis=0, concat_axis=0, tiled=True)


def trade(part, flip):
    return lax.ppermute(part, "prompt", [(i, i ^ flip) for i in range(4)])


def local(answer_qkv, prefix_kv, reveal_qkv, reveal_places):
    packed, select, *parts = pack(
        reveal_places.reshape(1, REV),
        answer_qkv.transpose(0, 2, 1, 3),
        reveal_qkv.transpose(0, 2, 1, 3),
        prefix_kv,
    )
    parts = [trade(part, flip) for part, flip in zip(parts, FLIPS)]
    grouped = exchange(packed)
    turned = exchange(attend(grouped, *arrange_prefix(parts, prefix_kv)))
    return place_outputs(turned, select)


def solution(mesh):
    placed = (
        P("prompt", "sample", None, None),
        P(None, "prompt", None, "sample"),
        P("prompt", "sample", None, None),
        P("prompt", "sample", None),
    )
    return jax.shard_map(
        local,
        mesh=mesh,
        in_specs=placed,
        out_specs=(P("prompt", "sample", None), P("prompt", "sample", None)),
        check_vma=False,
    )
```

profile of v0, /device:TPU:0, one launch (start us, length us, event | category | flops | bytes accessed | tf_op | source)
XLA Modules:
  0.0 138.0 jit_solution(2488126351820810842)
XLA Ops:
  0.6 4.3 %pack.1 = (bf16[32,3,144,128]{3,2,1,0:T(8,128)(2,1)}, bf16[128,128]{1,0:T(8,128)(2,1)}, bf16[512,2,128]{2,1,0:T(2,128)(2,1)}, bf16[512,2,128]{2,1,0:T(2,128)(2,1)}, bf16[512,2,128]{2,1,0:T(2,128)(2,1)}) custom-call(s32[1,16]{1,0:T(1,128)} %bitcast.5, bf16[1,3,128,4096]{3,2,1,0:T(8,128)(2,1)} %bitcast.3, bf16[1,3,16,4096]{3,2,1,0:T(8,128)(2,1)} %bitcast.4, ...), custom_call_target="tpu_custom_call" | custom-call | tf_op jit(solution)/shard_map/pack/pallas_call | solution.py:222
  5.0 3.5 %collective-permute-start = (bf16[512,2,128]{2,1,0:T(2,128)(2,1)}, bf16[512,2,128]{2,1,0:T(2,128)(2,1)S(1)}, u32[]{:S(2)}, u32[]{:S(2)}) collective-permute-start(bf16[512,2,128]{2,1,0:T(2,128)(2,1)} %get-tuple-element.10), channel_id=1, source_target_pairs={{0,96},{32,64},{64,32},{96,0},{1,97},{33,65},{65,33},{97,1},{2,98}... | collective-permute-start | bytes 786440 | tf_op jit(solution)/shard_map/ppermute | solution.py:291
  8.5 0.6 collective-permute-start.1
  9.1 0.0 collective-permute-start.2
  9.1 8.2 %all-to-all-start = ((bf16[32,3,144,128]{3,2,1,0:T(8,128)(2,1)}), bf16[32,3,144,128]{3,2,1,0:T(8,128)(2,1)}, u32[]{:S(2)}, u32[]{:S(2)}) async-start(bf16[32,3,144,128]{3,2,1,0:T(8,128)(2,1)} %get-tuple-element.9), calls=%async_computation | async-start | bytes 7077888 | tf_op jit(solution)/shard_map/all_to_all | solution.py:287
  17.3 0.0 collective-permute-done.refs_0_
  17.3 0.0 copy-start
  17.3 3.8 %collective-permute-done.1.refs_1_ = bf16[512,2,128]{2,1,0:T(2,128)(2,1)S(1)} collective-permute-done((bf16[512,2,128]{2,1,0:T(2,128)(2,1)}, bf16[512,2,128]{2,1,0:T(2,128)(2,1)S(1)}, u32[]{:S(2)}, u32[]{:S(2)}) %collective-permute-start.1) | collective-permute-done | bytes 262176 | tf_op jit(solution)/shard_map/ppermute | solution.py:291
  21.1 0.0 copy-start.1
  21.1 0.0 collective-permute-done.2.refs_2_
  21.2 0.0 copy-done
  21.2 0.7 copy-done.1
  21.8 0.0 copy-start.2
  21.8 0.7 copy-done.2
  22.6 6.5 %prefix.1 = (bf16[2048,128]{1,0:T(8,128)(2,1)}, bf16[144,2048]{1,0:T(8,128)(2,1)}) custom-call(bf16[512,2,128]{2,1,0:T(2,128)(2,1)} %copy-done, bf16[512,2,128]{2,1,0:T(2,128)(2,1)} %copy-done.1, bf16[512,2,128]{2,1,0:T(2,128)(2,1)} %copy-done.2, bf16[4,512,2,128]{3,2,1,0:T(2,128)(2,1)} %refs_3_.1), custom_call_target="tpu_custom_call" | custom-call | flops 60000002048 | bytes 2000000 | tf_op jit(solution)/shard_map/prefix/pallas_call | solution.py:266
  29.1 37.8 %all-to-all-done.qkv_ref = bf16[32,3,144,128]{3,2,1,0:T(8,128)(2,1)} async-done(((bf16[32,3,144,128]{3,2,1,0:T(8,128)(2,1)}), bf16[32,3,144,128]{3,2,1,0:T(8,128)(2,1)}, u32[]{:S(2)}, u32[]{:S(2)}) %all-to-all-start) | async-done | bytes 3538976 | tf_op jit(solution)/shard_map/all_to_all | solution.py:287
  66.9 34.2 %attend.1 = bf16[32,2,128,128]{3,2,1,0:T(8,128)(2,1)} custom-call(bf16[32,3,144,128]{3,2,1,0:T(8,128)(2,1)} %all-to-all-done.qkv_ref, bf16[2048,128]{1,0:T(8,128)(2,1)} %get-tuple-element.13.kp_ref, bf16[144,2048]{1,0:T(8,128)(2,1)} %get-tuple-element.14.vpt_ref), custom_call_target="tpu_custom_call" | custom-call | flops 14000000000 | bytes 7000000 | tf_op jit(solution)/shard_map/attend/pallas_call | solution.py:119
  101.1 34.0 %all_to_all.10.turned_ref = bf16[32,2,128,128]{3,2,1,0:T(8,128)(2,1)} all-to-all(bf16[32,2,128,128]{3,2,1,0:T(8,128)(2,1)} %attend.1), channel_id=1, replica_groups=mesh['prompt'=4,'sample'=32] {'sample'}, dimensions={0} | all-to-all | bytes 4194304 | tf_op jit(solution)/shard_map/all_to_all | solution.py:287
  135.1 2.9 %place.1 = (bf16[1,128,4096]{2,1,0:T(8,128)(2,1)}, bf16[1,128,4096]{2,1,0:T(8,128)(2,1)}) custom-call(bf16[32,2,128,128]{3,2,1,0:T(8,128)(2,1)} %all_to_all.10.turned_ref, bf16[128,128]{1,0:T(8,128)(2,1)} %get-tuple-element.15.select_ref), custom_call_target="tpu_custom_call" | custom-call | tf_op jit(solution)/shard_map/place/pallas_call | solution.py:153
Async XLA Ops:
  5.0 12.3 %collective-permute-start = (bf16[512,2,128]{2,1,0:T(2,128)(2,1)}, bf16[512,2,128]{2,1,0:T(2,128)(2,1)S(1)}, u32[]{:S(2)}, u32[]{:S(2)}) collective-permute-start(bf16[512,2,128]{2,1,0:T(2,128)(2,1)} %get-tuple-element.10), channel_id=1, source_target_pairs={{0,96},{32,64},{64,32},{96,0},{1,97},{33,65},{65,33},{97,1},{2,98}... | collective-permute-start | bytes 786440 | tf_op jit(solution)/shard_map/ppermute | solution.py:291
  8.5 12.7 %collective-permute-start.1 = (bf16[512,2,128]{2,1,0:T(2,128)(2,1)}, bf16[512,2,128]{2,1,0:T(2,128)(2,1)S(1)}, u32[]{:S(2)}, u32[]{:S(2)}) collective-permute-start(bf16[512,2,128]{2,1,0:T(2,128)(2,1)} %get-tuple-element.11), channel_id=1, source_target_pairs={{0,64},{32,96},{64,0},{96,32},{1,65},{33,97},{65,1},{97,33},{2,66}... | collective-permute-start | bytes 786440 | tf_op jit(solution)/shard_map/ppermute | solution.py:291
  9.1 12.1 %collective-permute-start.2 = (bf16[512,2,128]{2,1,0:T(2,128)(2,1)}, bf16[512,2,128]{2,1,0:T(2,128)(2,1)S(1)}, u32[]{:S(2)}, u32[]{:S(2)}) collective-permute-start(bf16[512,2,128]{2,1,0:T(2,128)(2,1)} %get-tuple-element.12), channel_id=1, source_target_pairs={{0,32},{32,0},{64,96},{96,64},{1,33},{33,1},{65,97},{97,65},{2,34}... | collective-permute-start | bytes 786440 | tf_op jit(solution)/shard_map/ppermute | solution.py:291
  9.1 57.7 %all-to-all-start = ((bf16[32,3,144,128]{3,2,1,0:T(8,128)(2,1)}), bf16[32,3,144,128]{3,2,1,0:T(8,128)(2,1)}, u32[]{:S(2)}, u32[]{:S(2)}) async-start(bf16[32,3,144,128]{3,2,1,0:T(8,128)(2,1)} %get-tuple-element.9), calls=%async_computation | async-start | bytes 7077888 | tf_op jit(solution)/shard_map/all_to_all | solution.py:287
  17.3 3.9 %copy-start = (bf16[512,2,128]{2,1,0:T(2,128)(2,1)}, bf16[512,2,128]{2,1,0:T(2,128)(2,1)S(1)}, u32[]{:S(2)}) copy-start(bf16[512,2,128]{2,1,0:T(2,128)(2,1)S(1)} %collective-permute-done.refs_0_) | copy-start | bytes 786436
  21.1 0.7 copy-start.1
  21.8 0.7 copy-start.2
where the time goes:
time: 138 us
  Pallas kernels  48 us (35%)
  waiting for transfers between devices  41.6 us (30%)
  blocking collectives  34 us (25%)
  starting transfers between devices  12.3 us (9%)
  local copies, waits for them, and re-layouts  1.41 us (1%)
    all_to_all x1, waiting for transfers between devices, exchange(): lax.all_to_all(array, 'sample', split_axis=0, concat_axis=0, tiled=True)  37.8 us
    pallas_call x1, Pallas kernels, attend(): pl.pallas_call(attend_kernel, grid=(samples,), in_specs=[pl.BlockSpec((SE...  34.2 us
    all_to_all x1, blocking collectives, exchange(): lax.all_to_all(array, 'sample', split_axis=0, concat_axis=0, tiled=True)  34 us
    all_to_all x1, starting transfers between devices, exchange(): lax.all_to_all(array, 'sample', split_axis=0, concat_axis=0, tiled=True)  8.16 us
    pallas_call x1, Pallas kernels, arrange_prefix(): pl.pallas_call(prefix_kernel, in_specs=[vmem] * len(parts) + [pl.BlockSpe...  6.5 us
    pallas_call x1, Pallas kernels, pack(): pl.pallas_call(functools.partial(pack_kernel, heads), grid=(count // head...  4.34 us
    ppermute x3, starting transfers between devices, trade(): return lax.ppermute(part, 'prompt', [(i, i ^ flip) for i in range(4)])  4.14 us
    ppermute x3, waiting for transfers between devices, trade(): return lax.ppermute(part, 'prompt', [(i, i ^ flip) for i in range(4)])  3.85 us
  transfers between devices with their start and end apart: 4, of which 2 were waited for; matrix products, arithmetic and copies ran while one was open for 0% of the time, Pallas kernels for 5%

commit v1 on v0

--- a/solution.py
+++ b/solution.py
@@ -26,6 +26,8 @@
 VMEM_LIMIT = 63 * 2**20
 FIRST = 128
 SPAN = 4
+GROUP = 2
+PLACE_LIMIT = 20 * 2**20
 PREFIX_COST = 60_000_000_000
 
 
@@ -41,92 +43,124 @@
     return jnp.exp2((scores - reference_row) * RATE).astype(jnp.bfloat16)
 
 
-def attend_kernel(qkv_ref, kp_ref, vpt_ref, out_ref, queries_ref):
-    queries_ref[: SEGS * SEG] = qkv_ref[:, 0, :SEG].reshape(SEGS * SEG, HEAD_DIM)
-    queries_ref[SEGS * SEG :] = qkv_ref[:, 0, SEG:].reshape(SEGS * REV, HEAD_DIM)
-
-    def answer_rows(kind, segs, rows):
-        picked = qkv_ref[segs, kind, rows]
-        return picked.reshape(picked.shape[0] * picked.shape[1], HEAD_DIM)
+def attend_kernel(group, qkv_ref, kp_ref, vpt_ref, out_ref, queries_ref, total_ref):
+    for sample in range(group):
+        segs = slice(sample * SEGS, (sample + 1) * SEGS)
+        at = sample * QUERIES
+        queries_ref[at : at + SEGS * SEG] = qkv_ref[segs, 0, :SEG].reshape(-1, HEAD_DIM)
+        queries_ref[at + SEGS * SEG : at + QUERIES] = qkv_ref[segs, 0, SEG:].reshape(-1, HEAD_DIM)
 
     def weighted(values, weights):
         ones = jnp.ones((AUG - HEAD_DIM, values.shape[0]), jnp.bfloat16)
         turned = jnp.concatenate([values.T, ones], axis=0)
         return jnp.dot(turned, weights, preferred_element_type=jnp.float32)
 
-    def attend(common_row, one_row, two_row, scale_one, scale_two):
-        queries = queries_ref[...]
-        total = None
-        common_max = None
-        for start in range(0, PREFIX, CHUNK):
-            scores = scores_of(kp_ref[start : start + CHUNK], queries)
-            folded = fold_max(scores)
-            common_max = folded if common_max is None else jnp.maximum(common_max, folded)
-            part = jnp.dot(
-                vpt_ref[:, start : start + CHUNK],
-                weigh(scores, common_row),
-                preferred_element_type=jnp.float32,
-            )
-            total = part if total is None else total + part
-        for start in range(0, SEGS, SPAN):
-            segs = slice(start, start + SPAN)
-            scores = scores_of(answer_rows(1, segs, slice(0, KEPT)), queries)
-            common_max = jnp.maximum(common_max, fold_max(scores))
-            total += weighted(answer_rows(2, segs, slice(0, KEPT)), weigh(scores, common_row))
-
-        def step(rows, row, scale):
-            scores = scores_of(answer_rows(1, slice(0, SEGS), rows), queries)
-            own = weighted(answer_rows(2, slice(0, SEGS), rows), weigh(scores, row))
-            own += total if scale is None else total * scale
-            return own[:HEAD_DIM] * (1.0 / own[HEAD_DIM : HEAD_DIM + 1]), fold_max(scores)
-
-        one, one_max = step(slice(KEPT, SEG), one_row, scale_one)
-        two, two_max = step(slice(SEG, ROWS), two_row, scale_two)
+    def answer_rows(kind, first_seg, segs, rows):
+        return qkv_ref[first_seg : first_seg + segs, kind, rows].reshape(-1, HEAD_DIM)
+
+    def step(sample, total, rows, row):
+        queries = queries_ref[sample * QUERIES : (sample + 1) * QUERIES]
+        scores = scores_of(answer_rows(1, sample * SEGS, SEGS, rows), queries)
+        own = weighted(answer_rows(2, sample * SEGS, SEGS, rows), weigh(scores, row)) + total
+        return own[:HEAD_DIM] * (1.0 / own[HEAD_DIM : HEAD_DIM + 1]), fold_max(scores)
+
+    def store(sample, one, two):
         renewed = two[:, SEGS * SEG :]
         lane = lax.broadcasted_iota(jnp.int32, (HEAD_DIM, SEG), 1)
         for seg in range(SEGS):
             lanes = slice(seg * SEG, (seg + 1) * SEG)
-            out_ref[seg, 0] = one[:, lanes].astype(jnp.bfloat16)
+            out_ref[sample * SEGS + seg, 0] = one[:, lanes].astype(jnp.bfloat16)
             shift = (KEPT - seg * REV) % SEG
             moved = pltpu.roll(renewed, shift, 1) if shift else renewed
-            out_ref[seg, 1] = jnp.where(lane < KEPT, two[:, lanes], moved).astype(jnp.bfloat16)
-        return common_max, one_max, two_max
-
-    first = scores_of(kp_ref[:FIRST], queries_ref[...])
-    start_row = jnp.max(first, axis=0, keepdims=True)
-    common_max, one_max, two_max = attend(start_row, start_row, start_row, None, None)
-    largest = jnp.maximum(common_max, jnp.maximum(one_max, two_max))
-    excess = jnp.max(largest - start_row) * RATE
-
-    @pl.when(excess > LIMIT)
+            merged = jnp.where(lane < KEPT, two[:, lanes], moved)
+            out_ref[sample * SEGS + seg, 1] = merged.astype(jnp.bfloat16)
+
+    queries = queries_ref[...]
+    start_row = jnp.max(scores_of(kp_ref[:FIRST], queries), axis=0, keepdims=True)
+    prefix_total = None
+    prefix_max = None
+    for start in range(0, PREFIX, CHUNK):
+        scores = scores_of(kp_ref[start : start + CHUNK], queries)
+        folded = fold_max(scores)
+        prefix_max = folded if prefix_max is None else jnp.maximum(prefix_max, folded)
+        part = jnp.dot(
+            vpt_ref[:, start : start + CHUNK],
+            weigh(scores, start_row),
+            preferred_element_type=jnp.float32,
+        )
+        prefix_total = part if prefix_total is None else prefix_total + part
+
+    largest = []
+    excess = None
+    for sample in range(group):
+        lanes = slice(sample * QUERIES, (sample + 1) * QUERIES)
+        row = start_row[:, lanes]
+        total = prefix_total[:, lanes]
+        common_max = prefix_max[:, lanes]
+        for start in range(0, SEGS, SPAN):
+            first_seg = sample * SEGS + start
+            scores = scores_of(answer_rows(1, first_seg, SPAN, slice(0, KEPT)), queries[lanes])
+            common_max = jnp.maximum(common_max, fold_max(scores))
+            total += weighted(
+                answer_rows(2, first_seg, SPAN, slice(0, KEPT)), weigh(scores, row)
+            )
+        one, one_max = step(sample, total, slice(KEPT, SEG), row)
+        two, two_max = step(sample, total, slice(SEG, ROWS), row)
+        store(sample, one, two)
+        largest.append((common_max, one_max, two_max))
+        above = jnp.maximum(common_max, jnp.maximum(one_max, two_max)) - row
+        excess = above if excess is None else jnp.maximum(excess, above)
+
+    @pl.when(jnp.max(excess) * RATE > LIMIT)
     def _():
-        common_row = jnp.max(common_max, axis=0, keepdims=True)
-        one_row = jnp.maximum(common_row, jnp.max(one_max, axis=0, keepdims=True))
-        two_row = jnp.maximum(common_row, jnp.max(two_max, axis=0, keepdims=True))
-        attend(
-            common_row,
-            one_row,
-            two_row,
-            jnp.exp2((common_row - one_row) * RATE),
-            jnp.exp2((common_row - two_row) * RATE),
-        )
+        for sample, (common_max, one_max, two_max) in enumerate(largest):
+            rows = slice(sample * QUERIES, (sample + 1) * QUERIES)
+            common_row = jnp.max(common_max, axis=0, keepdims=True)
+            one_row = jnp.maximum(common_row, jnp.max(one_max, axis=0, keepdims=True))
+            two_row = jnp.maximum(common_row, jnp.max(two_max, axis=0, keepdims=True))
+            total_ref[...] = jnp.zeros_like(total_ref)
+
+            def add_prefix(index, carry):
+                span = pl.ds(pl.multiple_of(index * FIRST, FIRST), FIRST)
+                weights = weigh(scores_of(kp_ref[span], queries_ref[rows]), common_row)
+                total_ref[...] += jnp.dot(
+                    vpt_ref[:, span], weights, preferred_element_type=jnp.float32
+                )
+                return carry
+
+            def add_answers(seg, carry):
+                scores = scores_of(qkv_ref[seg, 1, :KEPT], queries_ref[rows])
+                total_ref[...] += weighted(qkv_ref[seg, 2, :KEPT], weigh(scores, common_row))
+                return carry
+
+            lax.fori_loop(0, PREFIX // FIRST, add_prefix, 0)
+            lax.fori_loop(sample * SEGS, (sample + 1) * SEGS, add_answers, 0)
+            scale_one = jnp.exp2((common_row - one_row) * RATE)
+            scale_two = jnp.exp2((common_row - two_row) * RATE)
+            one, _ = step(sample, total_ref[...] * scale_one, slice(KEPT, SEG), one_row)
+            two, _ = step(sample, total_ref[...] * scale_two, slice(SEG, ROWS), two_row)
+            store(sample, one, two)
 
 
 def attend(qkv, prefix_keys, prefix_values):
     samples = qkv.shape[0] // SEGS
+    group = GROUP
     whole = lambda i: (0, 0)
     per = lambda i: (i, 0, 0, 0)
     return pl.pallas_call(
-        attend_kernel,
-        grid=(samples,),
+        functools.partial(attend_kernel, group),
+        grid=(samples // group,),
         in_specs=[
-            pl.BlockSpec((SEGS, 3, ROWS, HEAD_DIM), per),
+            pl.BlockSpec((group * SEGS, 3, ROWS, HEAD_DIM), per),
             pl.BlockSpec((PREFIX, HEAD_DIM), whole),
             pl.BlockSpec((AUG, PREFIX), whole),
         ],
-        out_specs=pl.BlockSpec((SEGS, 2, HEAD_DIM, SEG), per),
+        out_specs=pl.BlockSpec((group * SEGS, 2, HEAD_DIM, SEG), per),
         out_shape=jax.ShapeDtypeStruct((samples * SEGS, 2, HEAD_DIM, SEG), jnp.bfloat16),
-        scratch_shapes=[pltpu.VMEM((QUERIES, HEAD_DIM), jnp.bfloat16)],
+        scratch_shapes=[
+            pltpu.VMEM((group * QUERIES, HEAD_DIM), jnp.bfloat16),
+            pltpu.VMEM((AUG, QUERIES), jnp.float32),
+        ],
         compiler_params=pltpu.CompilerParams(vmem_limit_bytes=VMEM_LIMIT),
         cost_estimate=pl.CostEstimate(
             flops=14_000_000_000, bytes_accessed=7_000_000, transcendentals=15_000_000
@@ -159,7 +193,7 @@
         ],
         out_specs=[spec, spec],
         out_shape=[shape, shape],
-        compiler_params=pltpu.CompilerParams(vmem_limit_bytes=VMEM_LIMIT),
+        compiler_params=pltpu.CompilerParams(vmem_limit_bytes=PLACE_LIMIT),
         name="place",
     )(turned, select)
 

time: 138 us -> 168 us (1.22)
  Pallas kernels: 48 us -> 77.8 us
    pallas_call x1, Pallas kernels: 34.2 us -> 65.2 us  [attend(): pl.pallas_call(functools.partial(attend_kernel, group), grid=(samples //...]
  transfers between devices with their start and end apart: 4 -> 4, of which waited for: 2 -> 2; matrix products, arithmetic and copies ran while one was open for 0% -> 0% of each run, Pallas kernels for 5% -> 4%
where the time goes in v1:
time: 168 us
  Pallas kernels  77.8 us (46%)
  waiting for transfers between devices  41.6 us (25%)
  blocking collectives  34 us (20%)
  starting transfers between devices  12.3 us (7%)
    pallas_call x1, Pallas kernels, attend(): pl.pallas_call(functools.partial(attend_kernel, group), grid=(samples //...  65.2 us
    all_to_all x1, waiting for transfers between devices, exchange(): lax.all_to_all(array, 'sample', split_axis=0, concat_axis=0, tiled=True)  37.8 us
    all_to_all x1, blocking collectives, exchange(): lax.all_to_all(array, 'sample', split_axis=0, concat_axis=0, tiled=True)  34 us
    all_to_all x1, starting transfers between devices, exchange(): lax.all_to_all(array, 'sample', split_axis=0, concat_axis=0, tiled=True)  8.16 us
    pallas_call x1, Pallas kernels, arrange_prefix(): pl.pallas_call(prefix_kernel, in_specs=[vmem] * len(parts) + [pl.BlockSpe...  6.5 us
    pallas_call x1, Pallas kernels, pack(): pl.pallas_call(functools.partial(pack_kernel, heads), grid=(count // head...  4.32 us
    ppermute x3, starting transfers between devices, trade(): return lax.ppermute(part, 'prompt', [(i, i ^ flip) for i in range(4)])  4.14 us
    ppermute x3, waiting for transfers between devices, trade(): return lax.ppermute(part, 'prompt', [(i, i ^ flip) for i in range(4)])  3.85 us
  transfers between devices with their start and end apart: 4, of which 2 were waited for; matrix products, arithmetic and copies ran while one was open for 0% of the time, Pallas kernels for 4%

profile of v1, /device:TPU:0, one launch (start us, length us, event | category | flops | bytes accessed | tf_op | source)
XLA Modules:
  0.0 167.8 jit_solution(18118675691685119555)
XLA Ops:
  0.6 4.3 %pack.1 = (bf16[32,3,144,128]{3,2,1,0:T(8,128)(2,1)}, bf16[128,128]{1,0:T(8,128)(2,1)}, bf16[512,2,128]{2,1,0:T(2,128)(2,1)}, bf16[512,2,128]{2,1,0:T(2,128)(2,1)}, bf16[512,2,128]{2,1,0:T(2,128)(2,1)}) custom-call(s32[1,16]{1,0:T(1,128)} %bitcast.5, bf16[1,3,128,4096]{3,2,1,0:T(8,128)(2,1)} %bitcast.3, bf16[1,3,16,4096]{3,2,1,0:T(8,128)(2,1)} %bitcast.4, ...), custom_call_target="tpu_custom_call" | custom-call | tf_op jit(solution)/shard_map/pack/pallas_call | solution.py:256
  5.0 3.5 %collective-permute-start = (bf16[512,2,128]{2,1,0:T(2,128)(2,1)}, bf16[512,2,128]{2,1,0:T(2,128)(2,1)S(1)}, u32[]{:S(2)}, u32[]{:S(2)}) collective-permute-start(bf16[512,2,128]{2,1,0:T(2,128)(2,1)} %get-tuple-element.10), channel_id=1, source_target_pairs={{0,96},{32,64},{64,32},{96,0},{1,97},{33,65},{65,33},{97,1},{2,98}... | collective-permute-start | bytes 786440 | tf_op jit(solution)/shard_map/ppermute | solution.py:325
  8.4 0.6 collective-permute-start.1
  9.1 0.0 collective-permute-start.2
  9.1 8.2 %all-to-all-start = ((bf16[32,3,144,128]{3,2,1,0:T(8,128)(2,1)}), bf16[32,3,144,128]{3,2,1,0:T(8,128)(2,1)}, u32[]{:S(2)}, u32[]{:S(2)}) async-start(bf16[32,3,144,128]{3,2,1,0:T(8,128)(2,1)} %get-tuple-element.9), calls=%async_computation | async-start | bytes 7077888 | tf_op jit(solution)/shard_map/all_to_all | solution.py:321
  17.3 0.0 collective-permute-done.refs_0_
  17.3 0.0 copy-start.1
  17.3 3.8 %collective-permute-done.1.refs_1_ = bf16[512,2,128]{2,1,0:T(2,128)(2,1)S(1)} collective-permute-done((bf16[512,2,128]{2,1,0:T(2,128)(2,1)}, bf16[512,2,128]{2,1,0:T(2,128)(2,1)S(1)}, u32[]{:S(2)}, u32[]{:S(2)}) %collective-permute-start.1) | collective-permute-done | bytes 262176 | tf_op jit(solution)/shard_map/ppermute | solution.py:325
  21.1 0.0 copy-start.2
  21.1 0.0 collective-permute-done.2.refs_2_
  21.1 0.0 copy-done.1
  21.1 0.7 copy-done.2
  21.8 0.0 copy-start.3
  21.8 0.7 copy-done.3
  22.5 6.5 %prefix.1 = (bf16[2048,128]{1,0:T(8,128)(2,1)}, bf16[144,2048]{1,0:T(8,128)(2,1)}) custom-call(bf16[512,2,128]{2,1,0:T(2,128)(2,1)} %copy-done.1, bf16[512,2,128]{2,1,0:T(2,128)(2,1)} %copy-done.2, bf16[512,2,128]{2,1,0:T(2,128)(2,1)} %copy-done.3, bf16[4,512,2,128]{3,2,1,0:T(2,128)(2,1)} %refs_3_.1), custom_call_target="tpu_custom_call" | custom-call | flops 60000002048 | bytes 2000000 | tf_op jit(solution)/shard_map/prefix/pallas_call | solution.py:300
  29.1 37.8 %all-to-all-done.qkv_ref = bf16[32,3,144,128]{3,2,1,0:T(8,128)(2,1)} async-done(((bf16[32,3,144,128]{3,2,1,0:T(8,128)(2,1)}), bf16[32,3,144,128]{3,2,1,0:T(8,128)(2,1)}, u32[]{:S(2)}, u32[]{:S(2)}) %all-to-all-start) | async-done | bytes 3538976 | tf_op jit(solution)/shard_map/all_to_all | solution.py:321
  66.8 65.2 %attend.1 = bf16[32,2,128,128]{3,2,1,0:T(8,128)(2,1)} custom-call(bf16[32,3,144,128]{3,2,1,0:T(8,128)(2,1)} %all-to-all-done.qkv_ref, bf16[2048,128]{1,0:T(8,128)(2,1)} %get-tuple-element.13.kp_ref, bf16[144,2048]{1,0:T(8,128)(2,1)} %get-tuple-element.14.vpt_ref), custom_call_target="tpu_custom_call" | custom-call | flops 14000000000 | bytes 7000000 | tf_op jit(solution)/shard_map/attend/pallas_call | solution.py:150
  132.1 0.0 copy-start
  132.1 34.0 %all_to_all.10.turned_ref = bf16[32,2,128,128]{3,2,1,0:T(8,128)(2,1)S(1)} all-to-all(bf16[32,2,128,128]{3,2,1,0:T(8,128)(2,1)} %attend.1), channel_id=1, replica_groups=mesh['prompt'=4,'sample'=32] {'sample'}, dimensions={0} | all-to-all | bytes 4194304 | tf_op jit(solution)/shard_map/all_to_all | solution.py:321
  166.1 0.0 copy-done
  166.1 1.7 %place.1 = (bf16[1,128,4096]{2,1,0:T(8,128)(2,1)}, bf16[1,128,4096]{2,1,0:T(8,128)(2,1)}) custom-call(bf16[32,2,128,128]{3,2,1,0:T(8,128)(2,1)S(1)} %all_to_all.10.turned_ref, bf16[128,128]{1,0:T(8,128)(2,1)S(1)} %copy-done), custom_call_target="tpu_custom_call" | custom-call | tf_op jit(solution)/shard_map/place/pallas_call | solution.py:187
Async XLA Ops:
  5.0 12.3 %collective-permute-start = (bf16[512,2,128]{2,1,0:T(2,128)(2,1)}, bf16[512,2,128]{2,1,0:T(2,128)(2,1)S(1)}, u32[]{:S(2)}, u32[]{:S(2)}) collective-permute-start(bf16[512,2,128]{2,1,0:T(2,128)(2,1)} %get-tuple-element.10), channel_id=1, source_target_pairs={{0,96},{32,64},{64,32},{96,0},{1,97},{33,65},{65,33},{97,1},{2,98}... | collective-permute-start | bytes 786440 | tf_op jit(solution)/shard_map/ppermute | solution.py:325
  8.4 12.7 %collective-permute-start.1 = (bf16[512,2,128]{2,1,0:T(2,128)(2,1)}, bf16[512,2,128]{2,1,0:T(2,128)(2,1)S(1)}, u32[]{:S(2)}, u32[]{:S(2)}) collective-permute-start(bf16[512,2,128]{2,1,0:T(2,128)(2,1)} %get-tuple-element.11), channel_id=1, source_target_pairs={{0,64},{32,96},{64,0},{96,32},{1,65},{33,97},{65,1},{97,33},{2,66}... | collective-permute-start | bytes 786440 | tf_op jit(solution)/shard_map/ppermute | solution.py:325
  9.1 12.1 %collective-permute-start.2 = (bf16[512,2,128]{2,1,0:T(2,128)(2,1)}, bf16[512,2,128]{2,1,0:T(2,128)(2,1)S(1)}, u32[]{:S(2)}, u32[]{:S(2)}) collective-permute-start(bf16[512,2,128]{2,1,0:T(2,128)(2,1)} %get-tuple-element.12), channel_id=1, source_target_pairs={{0,32},{32,0},{64,96},{96,64},{1,33},{33,1},{65,97},{97,65},{2,34}... | collective-permute-start | bytes 786440 | tf_op jit(solution)/shard_map/ppermute | solution.py:325
  9.1 57.7 %all-to-all-start = ((bf16[32,3,144,128]{3,2,1,0:T(8,128)(2,1)}), bf16[32,3,144,128]{3,2,1,0:T(8,128)(2,1)}, u32[]{:S(2)}, u32[]{:S(2)}) async-start(bf16[32,3,144,128]{3,2,1,0:T(8,128)(2,1)} %get-tuple-element.9), calls=%async_computation | async-start | bytes 7077888 | tf_op jit(solution)/shard_map/all_to_all | solution.py:321
  17.3 3.9 %copy-start.1 = (bf16[512,2,128]{2,1,0:T(2,128)(2,1)}, bf16[512,2,128]{2,1,0:T(2,128)(2,1)S(1)}, u32[]{:S(2)}) copy-start(bf16[512,2,128]{2,1,0:T(2,128)(2,1)S(1)} %collective-permute-done.refs_0_) | copy-start | bytes 786436
  21.1 0.7 copy-start.2
  21.8 0.7 copy-start.3
  132.1 34.0 %copy-start = (bf16[128,128]{1,0:T(8,128)(2,1)S(1)}, bf16[128,128]{1,0:T(8,128)(2,1)}, u32[]{:S(2)}) copy-start(bf16[128,128]{1,0:T(8,128)(2,1)} %get-tuple-element.15.select_ref) | copy-start | bytes 98308

commit v2 on v1

--- a/solution.py
+++ b/solution.py
@@ -28,6 +28,7 @@
 SPAN = 4
 GROUP = 2
 PLACE_LIMIT = 20 * 2**20
+ATTEND_LIMIT = 44 * 2**20
 PREFIX_COST = 60_000_000_000
 
 
@@ -161,7 +162,7 @@
             pltpu.VMEM((group * QUERIES, HEAD_DIM), jnp.bfloat16),
             pltpu.VMEM((AUG, QUERIES), jnp.float32),
         ],
-        compiler_params=pltpu.CompilerParams(vmem_limit_bytes=VMEM_LIMIT),
+        compiler_params=pltpu.CompilerParams(vmem_limit_bytes=ATTEND_LIMIT),
         cost_estimate=pl.CostEstimate(
             flops=14_000_000_000, bytes_accessed=7_000_000, transcendentals=15_000_000
         ),
@@ -309,7 +310,7 @@
             pltpu.VMEM(prefix.shape[1:], jnp.bfloat16),
             pltpu.SemaphoreType.DMA,
         ],
-        compiler_params=pltpu.CompilerParams(vmem_limit_bytes=VMEM_LIMIT),
+        compiler_params=pltpu.CompilerParams(vmem_limit_bytes=PLACE_LIMIT),
         cost_estimate=pl.CostEstimate(
             flops=PREFIX_COST, bytes_accessed=2_000_000, transcendentals=0
         ),

time: 168 us -> 167 us (level)
  Pallas kernels: 77.8 us -> 74 us
  local copies, waits for them, and re-layouts: 1.41 us -> 4.94 us
    unnamed x8 -> x12, local copies, waits for them, and re-layouts: 1.41 us -> 4.94 us
    pallas_call x1, Pallas kernels: 65.2 us -> 62.4 us  [attend(): pl.pallas_call(functools.partial(attend_kernel, group), grid=(samples //...]
  transfers between devices with their start and end apart: 4 -> 4, of which waited for: 2 -> 2; matrix products, arithmetic and copies ran while one was open for 0% -> 0% of each run, Pallas kernels for 4% -> 3%
where the time goes in v2:
time: 167 us; the launch traced here: 166 us
  Pallas kernels  74 us (44%)
  waiting for transfers between devices  40.9 us (24%)
  blocking collectives  33.7 us (20%)
  starting transfers between devices  12.2 us (7%)
  local copies, waits for them, and re-layouts  4.94 us (3%)
    pallas_call x1, Pallas kernels, attend(): pl.pallas_call(functools.partial(attend_kernel, group), grid=(samples //...  62.4 us
    all_to_all x1, waiting for transfers between devices, exchange(): lax.all_to_all(array, 'sample', split_axis=0, concat_axis=0, tiled=True)  36.9 us
    all_to_all x1, blocking collectives, exchange(): lax.all_to_all(array, 'sample', split_axis=0, concat_axis=0, tiled=True)  33.7 us
    all_to_all x1, starting transfers between devices, exchange(): lax.all_to_all(array, 'sample', split_axis=0, concat_axis=0, tiled=True)  8.05 us
    pallas_call x1, Pallas kernels, arrange_prefix(): pl.pallas_call(prefix_kernel, in_specs=[vmem] * len(parts) + [pl.BlockSpe...  5.53 us
    unnamed x12, local copies, waits for them, and re-layouts  4.94 us
    pallas_call x1, Pallas kernels, pack(): pl.pallas_call(functools.partial(pack_kernel, heads), grid=(count // head...  4.32 us
    ppermute x3, starting transfers between devices, trade(): return lax.ppermute(part, 'prompt', [(i, i ^ flip) for i in range(4)])  4.14 us
  transfers between devices with their start and end apart: 4, of which 2 were waited for; matrix products, arithmetic and copies ran while one was open for 0% of the time, Pallas kernels for 3%

profile of v2, /device:TPU:0, one launch (start us, length us, event | category | flops | bytes accessed | tf_op | source)
XLA Modules:
  0.0 166.5 jit_solution(15413914155561586798)
XLA Ops:
  0.6 4.3 %pack.1 = (bf16[32,3,144,128]{3,2,1,0:T(8,128)(2,1)}, bf16[128,128]{1,0:T(8,128)(2,1)}, bf16[512,2,128]{2,1,0:T(2,128)(2,1)}, bf16[512,2,128]{2,1,0:T(2,128)(2,1)}, bf16[512,2,128]{2,1,0:T(2,128)(2,1)}) custom-call(s32[1,16]{1,0:T(1,128)} %bitcast.5, bf16[1,3,128,4096]{3,2,1,0:T(8,128)(2,1)} %bitcast.3, bf16[1,3,16,4096]{3,2,1,0:T(8,128)(2,1)} %bitcast.4, ...), custom_call_target="tpu_custom_call" | custom-call | tf_op jit(solution)/shard_map/pack/pallas_call | solution.py:257
  5.0 3.5 %collective-permute-start = (bf16[512,2,128]{2,1,0:T(2,128)(2,1)}, bf16[512,2,128]{2,1,0:T(2,128)(2,1)}, u32[]{:S(2)}, u32[]{:S(2)}) collective-permute-start(bf16[512,2,128]{2,1,0:T(2,128)(2,1)} %get-tuple-element.10), channel_id=1, source_target_pairs={{0,96},{32,64},{64,32},{96,0},{1,97},{33,65},{65,33},{97,1},{2,98}... | collective-permute-start | bytes 786440 | tf_op jit(solution)/shard_map/ppermute | solution.py:326
  8.4 0.6 collective-permute-start.1
  9.1 0.0 collective-permute-start.2
  9.1 8.0 %all-to-all-start = ((bf16[32,3,144,128]{3,2,1,0:T(8,128)(2,1)}), bf16[32,3,144,128]{3,2,1,0:T(8,128)(2,1)S(1)}, u32[]{:S(2)}, u32[]{:S(2)}) async-start(bf16[32,3,144,128]{3,2,1,0:T(8,128)(2,1)} %get-tuple-element.9), calls=%async_computation | async-start | bytes 7077888 | tf_op jit(solution)/shard_map/all_to_all | solution.py:322
  17.2 0.0 collective-permute-done.refs_0_
  17.2 4.1 %collective-permute-done.1.refs_1_ = bf16[512,2,128]{2,1,0:T(2,128)(2,1)} collective-permute-done((bf16[512,2,128]{2,1,0:T(2,128)(2,1)}, bf16[512,2,128]{2,1,0:T(2,128)(2,1)}, u32[]{:S(2)}, u32[]{:S(2)}) %collective-permute-start.1) | collective-permute-done | bytes 262176 | tf_op jit(solution)/shard_map/ppermute | solution.py:326
  21.2 0.0 collective-permute-done.2.refs_2_
  21.2 0.0 copy-start
  21.2 1.2 copy-done
  22.5 5.5 %prefix.1 = (bf16[2048,128]{1,0:T(8,128)(2,1)S(1)}, bf16[144,2048]{1,0:T(8,128)(2,1)S(1)}) custom-call(bf16[512,2,128]{2,1,0:T(2,128)(2,1)} %collective-permute-done.refs_0_, bf16[512,2,128]{2,1,0:T(2,128)(2,1)} %collective-permute-done.1.refs_1_, bf16[512,2,128]{2,1,0:T(2,128)(2,1)} %collective-permute-done.2.refs_2_, bf16[4,512,2,128]{3,2,1,0:T(2,128)(2,1)S(1)} %copy-done), custom_call_target="tpu_custom_call" | custom-call | flops 60000002048 | bytes 2000000 | tf_op jit(solution)/shard_map/prefix/pallas_call | solution.py:301
  28.0 0.0 copy-start.2
  28.0 0.8 copy-done.2
  28.8 0.0 copy-start.4
  28.8 0.8 copy-done.4
  29.6 36.9 %all-to-all-done.qkv_ref = bf16[32,3,144,128]{3,2,1,0:T(8,128)(2,1)S(1)} async-done(((bf16[32,3,144,128]{3,2,1,0:T(8,128)(2,1)}), bf16[32,3,144,128]{3,2,1,0:T(8,128)(2,1)S(1)}, u32[]{:S(2)}, u32[]{:S(2)}) %all-to-all-start) | async-done | bytes 3538976 | tf_op jit(solution)/shard_map/all_to_all | solution.py:322
  66.5 0.0 copy-start.3
  66.5 1.1 copy-done.3
  67.5 0.0 copy-start.5
  67.5 1.0 copy-done.5
  68.6 62.4 %attend.1 = bf16[32,2,128,128]{3,2,1,0:T(8,128)(2,1)S(1)} custom-call(bf16[32,3,144,128]{3,2,1,0:T(8,128)(2,1)S(1)} %all-to-all-done.qkv_ref, bf16[2048,128]{1,0:T(8,128)(2,1)S(1)} %copy-done.5, bf16[144,2048]{1,0:T(8,128)(2,1)S(1)} %copy-done.3), custom_call_target="tpu_custom_call" | custom-call | flops 14000000000 | bytes 7000000 | tf_op jit(solution)/shard_map/attend/pallas_call | solution.py:151
  131.0 0.0 copy-start.1
  131.0 33.7 %all_to_all.10.turned_ref = bf16[32,2,128,128]{3,2,1,0:T(8,128)(2,1)S(1)} all-to-all(bf16[32,2,128,128]{3,2,1,0:T(8,128)(2,1)S(1)} %attend.1), channel_id=1, replica_groups=mesh['prompt'=4,'sample'=32] {'sample'}, dimensions={0} | all-to-all | bytes 4194304 | tf_op jit(solution)/shard_map/all_to_all | solution.py:322
  164.7 0.0 copy-done.1
  164.7 1.7 %place.1 = (bf16[1,128,4096]{2,1,0:T(8,128)(2,1)}, bf16[1,128,4096]{2,1,0:T(8,128)(2,1)}) custom-call(bf16[32,2,128,128]{3,2,1,0:T(8,128)(2,1)S(1)} %all_to_all.10.turned_ref, bf16[128,128]{1,0:T(8,128)(2,1)S(1)} %copy-done.1), custom_call_target="tpu_custom_call" | custom-call | tf_op jit(solution)/shard_map/place/pallas_call | solution.py:188
Async XLA Ops:
  5.0 12.2 %collective-permute-start = (bf16[512,2,128]{2,1,0:T(2,128)(2,1)}, bf16[512,2,128]{2,1,0:T(2,128)(2,1)}, u32[]{:S(2)}, u32[]{:S(2)}) collective-permute-start(bf16[512,2,128]{2,1,0:T(2,128)(2,1)} %get-tuple-element.10), channel_id=1, source_target_pairs={{0,96},{32,64},{64,32},{96,0},{1,97},{33,65},{65,33},{97,1},{2,98}... | collective-permute-start | bytes 786440 | tf_op jit(solution)/shard_map/ppermute | solution.py:326
  8.4 12.8 %collective-permute-start.1 = (bf16[512,2,128]{2,1,0:T(2,128)(2,1)}, bf16[512,2,128]{2,1,0:T(2,128)(2,1)}, u32[]{:S(2)}, u32[]{:S(2)}) collective-permute-start(bf16[512,2,128]{2,1,0:T(2,128)(2,1)} %get-tuple-element.11), channel_id=1, source_target_pairs={{0,64},{32,96},{64,0},{96,32},{1,65},{33,97},{65,1},{97,33},{2,66}... | collective-permute-start | bytes 786440 | tf_op jit(solution)/shard_map/ppermute | solution.py:326
  9.1 12.2 %collective-permute-start.2 = (bf16[512,2,128]{2,1,0:T(2,128)(2,1)}, bf16[512,2,128]{2,1,0:T(2,128)(2,1)}, u32[]{:S(2)}, u32[]{:S(2)}) collective-permute-start(bf16[512,2,128]{2,1,0:T(2,128)(2,1)} %get-tuple-element.12), channel_id=1, source_target_pairs={{0,32},{32,0},{64,96},{96,64},{1,33},{33,1},{65,97},{97,65},{2,34}... | collective-permute-start | bytes 786440 | tf_op jit(solution)/shard_map/ppermute | solution.py:326
  9.1 57.4 %all-to-all-start = ((bf16[32,3,144,128]{3,2,1,0:T(8,128)(2,1)}), bf16[32,3,144,128]{3,2,1,0:T(8,128)(2,1)S(1)}, u32[]{:S(2)}, u32[]{:S(2)}) async-start(bf16[32,3,144,128]{3,2,1,0:T(8,128)(2,1)} %get-tuple-element.9), calls=%async_computation | async-start | bytes 7077888 | tf_op jit(solution)/shard_map/all_to_all | solution.py:322
  21.2 1.2 copy-start
  28.0 0.8 copy-start.2
  28.8 0.8 copy-start.4
  66.5 1.1 copy-start.3
  67.5 1.0 copy-start.5
  131.0 33.8 %copy-start.1 = (bf16[128,128]{1,0:T(8,128)(2,1)S(1)}, bf16[128,128]{1,0:T(8,128)(2,1)}, u32[]{:S(2)}) copy-start(bf16[128,128]{1,0:T(8,128)(2,1)} %get-tuple-element.15.select_ref) | copy-start | bytes 98308

commit v3 on v2

--- a/solution.py
+++ b/solution.py
@@ -44,7 +44,7 @@
     return jnp.exp2((scores - reference_row) * RATE).astype(jnp.bfloat16)
 
 
-def attend_kernel(group, qkv_ref, kp_ref, vpt_ref, out_ref, queries_ref, total_ref):
+def attend_kernel(group, qkv_ref, prefix_ref, out_ref, queries_ref, total_ref):
     for sample in range(group):
         segs = slice(sample * SEGS, (sample + 1) * SEGS)
         at = sample * QUERIES
@@ -77,18 +77,14 @@
             out_ref[sample * SEGS + seg, 1] = merged.astype(jnp.bfloat16)
 
     queries = queries_ref[...]
-    start_row = jnp.max(scores_of(kp_ref[:FIRST], queries), axis=0, keepdims=True)
+    start_row = jnp.max(scores_of(prefix_ref[0, :FIRST], queries), axis=0, keepdims=True)
     prefix_total = None
     prefix_max = None
     for start in range(0, PREFIX, CHUNK):
-        scores = scores_of(kp_ref[start : start + CHUNK], queries)
+        scores = scores_of(prefix_ref[0, start : start + CHUNK], queries)
         folded = fold_max(scores)
         prefix_max = folded if prefix_max is None else jnp.maximum(prefix_max, folded)
-        part = jnp.dot(
-            vpt_ref[:, start : start + CHUNK],
-            weigh(scores, start_row),
-            preferred_element_type=jnp.float32,
-        )
+        part = weighted(prefix_ref[1, start : start + CHUNK], weigh(scores, start_row))
         prefix_total = part if prefix_total is None else prefix_total + part
 
     largest = []
@@ -123,10 +119,8 @@
 
             def add_prefix(index, carry):
                 span = pl.ds(pl.multiple_of(index * FIRST, FIRST), FIRST)
-                weights = weigh(scores_of(kp_ref[span], queries_ref[rows]), common_row)
-                total_ref[...] += jnp.dot(
-                    vpt_ref[:, span], weights, preferred_element_type=jnp.float32
-                )
+                weights = weigh(scores_of(prefix_ref[0, span], queries_ref[rows]), common_row)
+                total_ref[...] += weighted(prefix_ref[1, span], weights)
                 return carry
 
             def add_answers(seg, carry):
@@ -143,18 +137,16 @@
             store(sample, one, two)
 
 
-def attend(qkv, prefix_keys, prefix_values):
+def attend(qkv, prefix):
     samples = qkv.shape[0] // SEGS
     group = GROUP
-    whole = lambda i: (0, 0)
     per = lambda i: (i, 0, 0, 0)
     return pl.pallas_call(
         functools.partial(attend_kernel, group),
         grid=(samples // group,),
         in_specs=[
             pl.BlockSpec((group * SEGS, 3, ROWS, HEAD_DIM), per),
-            pl.BlockSpec((PREFIX, HEAD_DIM), whole),
-            pl.BlockSpec((AUG, PREFIX), whole),
+            pl.BlockSpec((2, PREFIX, HEAD_DIM), lambda i: (0, 0, 0)),
         ],
         out_specs=pl.BlockSpec((group * SEGS, 2, HEAD_DIM, SEG), per),
         out_shape=jax.ShapeDtypeStruct((samples * SEGS, 2, HEAD_DIM, SEG), jnp.bfloat16),
@@ -167,7 +159,7 @@
             flops=14_000_000_000, bytes_accessed=7_000_000, transcendentals=15_000_000
         ),
         name="attend",
-    )(qkv, prefix_keys, prefix_values)
+    )(qkv, prefix)
 
 
 def place_kernel(heads, turned_ref, select_ref, one_ref, two_ref):
@@ -283,17 +275,16 @@
 
 
 def prefix_kernel(*refs):
-    *parts, prefix_ref, keys_ref, values_ref, own_ref, sem = refs
+    *parts, prefix_ref, out_ref, own_ref, sem = refs
     copy = pltpu.make_async_copy(prefix_ref.at[lax.axis_index("prompt")], own_ref, sem)
     copy.start()
-    values_ref[HEAD_DIM:] = jnp.ones((AUG - HEAD_DIM, PREFIX), jnp.bfloat16)
     count = own_ref.shape[0]
     for index, part in enumerate((*parts, own_ref)):
         if part is own_ref:
             copy.wait()
         span = slice(index * count, (index + 1) * count)
-        keys_ref[span] = part[:, 0]
-        values_ref[:HEAD_DIM, span] = part[:, 1].T
+        out_ref[0, span] = part[:, 0]
+        out_ref[1, span] = part[:, 1]
 
 
 def arrange_prefix(parts, prefix):
@@ -301,11 +292,8 @@
     return pl.pallas_call(
         prefix_kernel,
         in_specs=[vmem] * len(parts) + [pl.BlockSpec(memory_space=pl.ANY)],
-        out_specs=[vmem] * 2,
-        out_shape=[
-            jax.ShapeDtypeStruct((PREFIX, HEAD_DIM), jnp.bfloat16),
-            jax.ShapeDtypeStruct((AUG, PREFIX), jnp.bfloat16),
-        ],
+        out_specs=vmem,
+        out_shape=jax.ShapeDtypeStruct((2, PREFIX, HEAD_DIM), jnp.bfloat16),
         scratch_shapes=[
             pltpu.VMEM(prefix.shape[1:], jnp.bfloat16),
             pltpu.SemaphoreType.DMA,
@@ -335,7 +323,7 @@
     )
     parts = [trade(part, flip) for part, flip in zip(parts, FLIPS)]
     grouped = exchange(packed)
-    turned = exchange(attend(grouped, *arrange_prefix(parts, prefix_kv)))
+    turned = exchange(attend(grouped, arrange_prefix(parts, prefix_kv)))
     return place_outputs(turned, select)
 
 

time: 167 us -> 166 us (level)
  waiting for transfers between devices: 40.9 us -> 43.1 us
  Pallas kernels: 74 us -> 72.1 us
    all_to_all x1, waiting for transfers between devices: 36.9 us -> 39 us  [exchange(): lax.all_to_all(array, 'sample', split_axis=0, concat_axis=0, tiled=True)]
    unnamed x12 -> x8, local copies, waits for them, and re-layouts: 4.94 us -> 3.42 us
  transfers between devices with their start and end apart: 4 -> 4, of which waited for: 2 -> 2; matrix products, arithmetic and copies ran while one was open for 0% -> 0% of each run, Pallas kernels for 3% -> 2%
where the time goes in v3:
time: 166 us; the launch traced here: 165 us
  Pallas kernels  72.1 us (43%)
  waiting for transfers between devices  43.1 us (26%)
  blocking collectives  33.7 us (20%)
  starting transfers between devices  12.2 us (7%)
  local copies, waits for them, and re-layouts  3.42 us (2%)
    pallas_call x1, Pallas kernels, attend(): pl.pallas_call(functools.partial(attend_kernel, group), grid=(samples //...  62.1 us
    all_to_all x1, waiting for transfers between devices, exchange(): lax.all_to_all(array, 'sample', split_axis=0, concat_axis=0, tiled=True)  39 us
    all_to_all x1, blocking collectives, exchange(): lax.all_to_all(array, 'sample', split_axis=0, concat_axis=0, tiled=True)  33.7 us
    all_to_all x1, starting transfers between devices, exchange(): lax.all_to_all(array, 'sample', split_axis=0, concat_axis=0, tiled=True)  8.05 us
    pallas_call x1, Pallas kernels, pack(): pl.pallas_call(functools.partial(pack_kernel, heads), grid=(count // head...  4.31 us
    ppermute x3, starting transfers between devices, trade(): return lax.ppermute(part, 'prompt', [(i, i ^ flip) for i in range(4)])  4.14 us
    ppermute x3, waiting for transfers between devices, trade(): return lax.ppermute(part, 'prompt', [(i, i ^ flip) for i in range(4)])  4.08 us
    pallas_call x1, Pallas kernels, arrange_prefix(): pl.pallas_call(prefix_kernel, in_specs=[vmem] * len(parts) + [pl.BlockSpe...  3.99 us
  transfers between devices with their start and end apart: 4, of which 2 were waited for; matrix products, arithmetic and copies ran while one was open for 0% of the time, Pallas kernels for 2%

profile of v3, /device:TPU:0, one launch (start us, length us, event | category | flops | bytes accessed | tf_op | source)
XLA Modules:
  0.0 165.3 jit_solution(9763883797685012707)
XLA Ops:
  0.6 4.3 %pack.1 = (bf16[32,3,144,128]{3,2,1,0:T(8,128)(2,1)}, bf16[128,128]{1,0:T(8,128)(2,1)}, bf16[512,2,128]{2,1,0:T(2,128)(2,1)}, bf16[512,2,128]{2,1,0:T(2,128)(2,1)}, bf16[512,2,128]{2,1,0:T(2,128)(2,1)}) custom-call(s32[1,16]{1,0:T(1,128)} %bitcast.5, bf16[1,3,128,4096]{3,2,1,0:T(8,128)(2,1)} %bitcast.3, bf16[1,3,16,4096]{3,2,1,0:T(8,128)(2,1)} %bitcast.4, ...), custom_call_target="tpu_custom_call" | custom-call | tf_op jit(solution)/shard_map/pack/pallas_call | solution.py:249
  4.9 3.5 %collective-permute-start = (bf16[512,2,128]{2,1,0:T(2,128)(2,1)}, bf16[512,2,128]{2,1,0:T(2,128)(2,1)}, u32[]{:S(2)}, u32[]{:S(2)}) collective-permute-start(bf16[512,2,128]{2,1,0:T(2,128)(2,1)} %get-tuple-element.8), channel_id=1, source_target_pairs={{0,96},{32,64},{64,32},{96,0},{1,97},{33,65},{65,33},{97,1},{2,98}... | collective-permute-start | bytes 786440 | tf_op jit(solution)/shard_map/ppermute | solution.py:314
  8.4 0.6 collective-permute-start.1
  9.1 0.0 collective-permute-start.2
  9.1 8.0 %all-to-all-start = ((bf16[32,3,144,128]{3,2,1,0:T(8,128)(2,1)}), bf16[32,3,144,128]{3,2,1,0:T(8,128)(2,1)S(1)}, u32[]{:S(2)}, u32[]{:S(2)}) async-start(bf16[32,3,144,128]{3,2,1,0:T(8,128)(2,1)} %get-tuple-element.7), calls=%async_computation | async-start | bytes 7077888 | tf_op jit(solution)/shard_map/all_to_all | solution.py:310
  17.1 0.0 collective-permute-done.refs_0_
  17.2 4.1 %collective-permute-done.1.refs_1_ = bf16[512,2,128]{2,1,0:T(2,128)(2,1)} collective-permute-done((bf16[512,2,128]{2,1,0:T(2,128)(2,1)}, bf16[512,2,128]{2,1,0:T(2,128)(2,1)}, u32[]{:S(2)}, u32[]{:S(2)}) %collective-permute-start.1) | collective-permute-done | bytes 262176 | tf_op jit(solution)/shard_map/ppermute | solution.py:314
  21.2 0.0 collective-permute-done.2.refs_2_
  21.2 0.0 copy-start
  21.2 1.2 copy-done
  22.5 4.0 %prefix.1.prefix_ref = bf16[2,2048,128]{2,1,0:T(8,128)(2,1)S(1)} custom-call(bf16[512,2,128]{2,1,0:T(2,128)(2,1)} %collective-permute-done.refs_0_, bf16[512,2,128]{2,1,0:T(2,128)(2,1)} %collective-permute-done.1.refs_1_, bf16[512,2,128]{2,1,0:T(2,128)(2,1)} %collective-permute-done.2.refs_2_, bf16[4,512,2,128]{3,2,1,0:T(2,128)(2,1)S(1)} %copy-done), custom_call_target="tpu_custom_call" | custom-call | flops 60000002048 | bytes 2000000 | tf_op jit(solution)/shard_map/prefix/pallas_call | solution.py:292
  26.5 0.0 copy-start.2
  26.5 1.0 copy-done.2
  27.4 39.0 %all-to-all-done.qkv_ref = bf16[32,3,144,128]{3,2,1,0:T(8,128)(2,1)S(1)} async-done(((bf16[32,3,144,128]{3,2,1,0:T(8,128)(2,1)}), bf16[32,3,144,128]{3,2,1,0:T(8,128)(2,1)S(1)}, u32[]{:S(2)}, u32[]{:S(2)}) %all-to-all-start) | async-done | bytes 3538976 | tf_op jit(solution)/shard_map/all_to_all | solution.py:310
  66.5 0.0 copy-start.3
  66.5 1.2 copy-done.3
  67.7 62.1 %attend.1 = bf16[32,2,128,128]{3,2,1,0:T(8,128)(2,1)S(1)} custom-call(bf16[32,3,144,128]{3,2,1,0:T(8,128)(2,1)S(1)} %all-to-all-done.qkv_ref, bf16[2,2048,128]{2,1,0:T(8,128)(2,1)S(1)} %copy-done.3), custom_call_target="tpu_custom_call" | custom-call | flops 14000000000 | bytes 7000000 | tf_op jit(solution)/shard_map/attend/pallas_call | solution.py:144
  129.8 0.0 copy-start.1
  129.8 33.7 %all_to_all.10.turned_ref = bf16[32,2,128,128]{3,2,1,0:T(8,128)(2,1)S(1)} all-to-all(bf16[32,2,128,128]{3,2,1,0:T(8,128)(2,1)S(1)} %attend.1), channel_id=1, replica_groups=mesh['prompt'=4,'sample'=32] {'sample'}, dimensions={0} | all-to-all | bytes 4194304 | tf_op jit(solution)/shard_map/all_to_all | solution.py:310
  163.6 0.0 copy-done.1
  163.6 1.7 %place.1 = (bf16[1,128,4096]{2,1,0:T(8,128)(2,1)}, bf16[1,128,4096]{2,1,0:T(8,128)(2,1)}) custom-call(bf16[32,2,128,128]{3,2,1,0:T(8,128)(2,1)S(1)} %all_to_all.10.turned_ref, bf16[128,128]{1,0:T(8,128)(2,1)S(1)} %copy-done.1), custom_call_target="tpu_custom_call" | custom-call | tf_op jit(solution)/shard_map/place/pallas_call | solution.py:180
Async XLA Ops:
  4.9 12.2 %collective-permute-start = (bf16[512,2,128]{2,1,0:T(2,128)(2,1)}, bf16[512,2,128]{2,1,0:T(2,128)(2,1)}, u32[]{:S(2)}, u32[]{:S(2)}) collective-permute-start(bf16[512,2,128]{2,1,0:T(2,128)(2,1)} %get-tuple-element.8), channel_id=1, source_target_pairs={{0,96},{32,64},{64,32},{96,0},{1,97},{33,65},{65,33},{97,1},{2,98}... | collective-permute-start | bytes 786440 | tf_op jit(solution)/shard_map/ppermute | solution.py:314
  8.4 12.8 %collective-permute-start.1 = (bf16[512,2,128]{2,1,0:T(2,128)(2,1)}, bf16[512,2,128]{2,1,0:T(2,128)(2,1)}, u32[]{:S(2)}, u32[]{:S(2)}) collective-permute-start(bf16[512,2,128]{2,1,0:T(2,128)(2,1)} %get-tuple-element.9), channel_id=1, source_target_pairs={{0,64},{32,96},{64,0},{96,32},{1,65},{33,97},{65,1},{97,33},{2,66}... | collective-permute-start | bytes 786440 | tf_op jit(solution)/shard_map/ppermute | solution.py:314
  9.1 12.2 %collective-permute-start.2 = (bf16[512,2,128]{2,1,0:T(2,128)(2,1)}, bf16[512,2,128]{2,1,0:T(2,128)(2,1)}, u32[]{:S(2)}, u32[]{:S(2)}) collective-permute-start(bf16[512,2,128]{2,1,0:T(2,128)(2,1)} %get-tuple-element.10), channel_id=1, source_target_pairs={{0,32},{32,0},{64,96},{96,64},{1,33},{33,1},{65,97},{97,65},{2,34}... | collective-permute-start | bytes 786440 | tf_op jit(solution)/shard_map/ppermute | solution.py:314
  9.1 57.4 %all-to-all-start = ((bf16[32,3,144,128]{3,2,1,0:T(8,128)(2,1)}), bf16[32,3,144,128]{3,2,1,0:T(8,128)(2,1)S(1)}, u32[]{:S(2)}, u32[]{:S(2)}) async-start(bf16[32,3,144,128]{3,2,1,0:T(8,128)(2,1)} %get-tuple-element.7), calls=%async_computation | async-start | bytes 7077888 | tf_op jit(solution)/shard_map/all_to_all | solution.py:310
  21.2 1.2 copy-start
  26.5 1.0 copy-start.2
  66.5 1.2 copy-start.3
  129.8 33.8 %copy-start.1 = (bf16[128,128]{1,0:T(8,128)(2,1)S(1)}, bf16[128,128]{1,0:T(8,128)(2,1)}, u32[]{:S(2)}) copy-start(bf16[128,128]{1,0:T(8,128)(2,1)} %get-tuple-element.11.select_ref) | copy-start | bytes 98308
